TPU v7x, 256 devices: a whole 4x4x8 slice. The times are simulated.
256 devices in a mesh: src: 16 (over y, x), tgt: 16 (over z, core).
Axes of the slice: x: 4, y: 4, z: 8, core: 2. Of those that a mesh axis runs over, the one named last changes fastest.
Arguments:
- log_kernel: bfloat16 [16, 16, 48, 256, 256], P('src', 'tgt'), may hold values from -8 to 320
- tile_rows: int32 [16, 16, 48], P('src', 'tgt'), may hold values from 0 to 127, as said below
- tile_cols: int32 [16, 16, 48], P('src', 'tgt'), may hold values from 0 to 127
- tile_count: int32 [16, 16], P('src', 'tgt'), may hold values from 1 to 48, as said below
- log_a: float32 [524288], P('src'), may hold values from -5 to 5
- log_b: float32 [524288], P('tgt'), may hold values from -5 to 5
- g_start: float32 [524288], P('tgt'), may hold values from -5 to 5
Outputs:
- source_pot: float32 [524288], P('src')
- target_pot: float32 [524288], P('tgt')
Inputs may be any that keep to these rules, and one draw needn't show every extreme that they name: `tile_rows`: the first tile_count slots of a device name distinct row and column block pairs; the live tiles of all devices together contain every source row and every target column; slots past tile_count hold ids that are not used. `tile_count`: some device has all 48 slots live.
All inputs are finite; a program needn't handle non-finite values.
Results may differ from a plain program's by a relative error of at most 0.0003.
Values sent between devices are 32-bit elements; how exact they have to be, the bound alone decides.
A program may use at most 64 MiB of HBM per device.

v0:
```python
import jax
import jax.numpy as jnp
from jax import lax
from jax.sharding import PartitionSpec as P

ITERS = 2


NEG = -1e30


def fold_blocks(tile_max, tile_sum, block_ids, is_live, nfold):
    onehot = (block_ids[:, None] == jnp.arange(nfold)[None, :]) & is_live[:, None]
    block_max = jnp.max(jnp.where(onehot[:, :, None], tile_max[:, None, :], NEG), axis=0)
    weight = onehot.astype(jnp.float32)
    spread = jnp.einsum("tr,rb->tb", weight, block_max, precision=lax.Precision.HIGHEST)
    scaled = tile_sum * jnp.exp(tile_max - spread)
    block_sum = jnp.einsum("tr,tb->rb", weight, scaled, precision=lax.Precision.HIGHEST)
    return (block_max, block_sum)


def tile_partials(kernel, fold_ids, pick_ids, is_live, vector, nfold, along_rows):
    selector = (pick_ids[:, None] == jnp.arange(vector.shape[0])[None, :]).astype(jnp.float32)
    selected = jnp.einsum("tc,cb->tb", selector, vector, precision=lax.Precision.HIGHEST)
    widened = kernel.astype(jnp.float32)
    if along_rows:
        shifted = widened + selected[:, None, :]
        reduce_axis = 2
    else:
        shifted = widened + selected[:, :, None]
        reduce_axis = 1
    tile_max = jnp.max(shifted, axis=reduce_axis)
    tile_sum = jnp.sum(jnp.exp(shifted - jnp.expand_dims(tile_max, reduce_axis)), axis=reduce_axis)
    tile_max = jnp.where(is_live[:, None], tile_max, NEG)
    tile_sum = jnp.where(is_live[:, None], tile_sum, 0.0)
    return fold_blocks(tile_max, tile_sum, fold_ids, is_live, nfold)


def local_pass(kernel, fold_ids, pick_ids, live_count, vector, nfold, along_rows):
    slots = kernel.shape[0]
    is_live = jnp.arange(slots) < live_count
    return tile_partials(kernel, fold_ids, pick_ids, is_live, vector, nfold, along_rows)


def settle_rows(block_max, block_sum, source_log):
    highest = lax.pmax(block_max, "tgt")
    summed = lax.psum(block_sum * jnp.exp(block_max - highest), "tgt")
    return source_log - (highest + jnp.log(summed))


def settle_cols(block_max, block_sum, target_log):
    highest = lax.pmax(block_max, "src")
    summed = lax.psum(block_sum * jnp.exp(block_max - highest), "src")
    return target_log - (highest + jnp.log(summed))


def per_device(log_kernel, tile_rows, tile_cols, tile_count, log_a, log_b, g_start):
    kernel = log_kernel[0, 0]
    row_ids = tile_rows[0, 0]
    col_ids = tile_cols[0, 0]
    live_count = tile_count[0, 0]
    width = kernel.shape[-1]
    row_blocks = log_a.shape[0] // width
    col_blocks = log_b.shape[0] // width
    source_log = log_a.reshape(row_blocks, width)
    target_log = log_b.reshape(col_blocks, width)
    target_pot = g_start.reshape(col_blocks, width)
    source_pot = source_log
    for sweep_index in range(ITERS):
        block_max, block_sum = local_pass(
            kernel, row_ids, col_ids, live_count, target_pot, row_blocks, True
        )
        source_pot = settle_rows(block_max, block_sum, source_log)
        block_max, block_sum = local_pass(
            kernel, col_ids, row_ids, live_count, source_pot, col_blocks, False
        )
        target_pot = settle_cols(block_max, block_sum, target_log)
    return (source_pot.reshape(-1), target_pot.reshape(-1))


def solution(mesh):
    in_specs = (
        P("src", "tgt", None, None, None),
        P("src", "tgt", None),
        P("src", "tgt", None),
        P("src", "tgt"),
        P("src"),
        P("tgt"),
        P("tgt"),
    )
    out_specs = (P("src"), P("tgt"))
    return jax.shard_map(
        per_device, mesh=mesh, in_specs=in_specs, out_specs=out_specs, check_vma=False
    )
```

profile of v0, /device:TPU:1, one launch (start us, length us, event | category | flops | bytes accessed | tf_op | source)
XLA Modules:
  0.0 881.0 jit_solution(17808289337946425235)
XLA Ops:
  10.5 4.5 fusion.1
  15.1 1.9 select_reduce_fusion.3
  17.1 5.8 fusion.15
  23.1 105.4 %all-reduce.9.cloned.1.call-done = f32[128,256]{1,0:T(8,128)} async-done(((f32[128,256]{1,0:T(8,128)}), f32[128,256]{1,0:T(8,128)}) %all-reduce.9.cloned.1.call-update) | async-done | bytes 131088 | tf_op jit(solution)/shard_map/pmax | solution.py:46
  128.6 1.9 convolution_multiply_fusion.3
  130.6 108.8 %all-reduce.11.cloned.1.call-done = f32[128,256]{1,0:T(8,128)} async-done(((f32[128,256]{1,0:T(8,128)}), f32[128,256]{1,0:T(8,128)}) %all-reduce.11.cloned.1.call-update) | async-done | bytes 131088 | tf_op jit(solution)/shard_map/psum | solution.py:47
  240.6 4.5 fusion.3
  245.1 5.2 fusion.13
  250.4 1.9 select_reduce_fusion.2
  253.6 90.2 %all-reduce.13.cloned.1.call-done = f32[128,256]{1,0:T(8,128)} async-done(((f32[128,256]{1,0:T(8,128)}), f32[128,256]{1,0:T(8,128)}) %all-reduce.13.cloned.1.call-update) | async-done | bytes 131088 | tf_op jit(solution)/shard_map/pmax | solution.py:52
  343.7 2.0 convolution_multiply_fusion.2
  345.8 93.7 %all-reduce.15.cloned.1.call-done = f32[128,256]{1,0:T(8,128)} async-done(((f32[128,256]{1,0:T(8,128)}), f32[128,256]{1,0:T(8,128)}) %all-reduce.15.cloned.1.call-update) | async-done | bytes 131088 | tf_op jit(solution)/shard_map/psum | solution.py:53
  440.7 4.5 fusion.5
  445.2 5.8 fusion.11
  451.1 1.9 select_reduce_fusion.1
  454.2 107.3 %all-reduce.17.cloned.1.call-done = f32[128,256]{1,0:T(8,128)} async-done(((f32[128,256]{1,0:T(8,128)}), f32[128,256]{1,0:T(8,128)}) %all-reduce.17.cloned.1.call-update) | async-done | bytes 131088 | tf_op jit(solution)/shard_map/pmax | solution.py:46
  561.6 2.0 convolution_multiply_fusion.1
  563.8 108.5 %all-reduce.19.cloned.1.call-done = f32[128,256]{1,0:T(8,128)} async-done(((f32[128,256]{1,0:T(8,128)}), f32[128,256]{1,0:T(8,128)}) %all-reduce.19.cloned.1.call-update) | async-done | bytes 131088 | tf_op jit(solution)/shard_map/psum | solution.py:47
  673.4 4.5 fusion.7
  678.0 5.2 fusion.9
  683.3 1.9 select_reduce_fusion
  686.4 90.2 %all-reduce.21.cloned.1.call-done = f32[128,256]{1,0:T(8,128)} async-done(((f32[128,256]{1,0:T(8,128)}), f32[128,256]{1,0:T(8,128)}) %all-reduce.21.cloned.1.call-update) | async-done | bytes 131088 | tf_op jit(solution)/shard_map/pmax | solution.py:52
  776.6 2.0 convolution_multiply_fusion
  779.3 93.2 %all-reduce.23.cloned.1.call-done = f32[128,256]{1,0:T(8,128)} async-done(((f32[128,256]{1,0:T(8,128)}), f32[128,256]{1,0:T(8,128)}) %all-reduce.23.cloned.1.call-update) | async-done | bytes 131088 | tf_op jit(solution)/shard_map/psum | solution.py:53
  (51 shorter events, 13.3 us)
Async XLA Ops:
  7.2 121.4 %all-reduce.9.cloned.1.call-start = ((), (), s32[]{:S(2)}) async-start(), calls=%async_computation | async-start | bytes 262144 | tf_op jit(solution)/shard_map/pmax | solution.py:46
  10.5 12.4 %copy-start.6 = (s32[1,1,48]{2,1,0:T(1,128)S(1)}, s32[1,1,48]{2,1,0:T(1,128)}, u32[]{:S(2)}) copy-start(s32[1,1,48]{2,1,0:T(1,128)} %param.8) | copy-start | bytes 580
  10.5 120.1 %copy-start.3 = (f32[32768]{0:T(1024)S(1)}, f32[32768]{0:T(1024)}, u32[]{:S(2)}) copy-start(f32[32768]{0:T(1024)} %param.11) | copy-start | bytes 393220
  17.0 5.9 copy-start
  17.0 222.4 %all-reduce.11.cloned.1.call-start = ((), (), s32[]{:S(2)}) async-start(), calls=%async_computation.1 | async-start | bytes 262144 | tf_op jit(solution)/shard_map/psum | solution.py:47
  130.5 213.2 %all-reduce.13.cloned.1.call-start = ((), (), s32[]{:S(2)}) async-start(), calls=%async_computation.2 | async-start | bytes 262144 | tf_op jit(solution)/shard_map/pmax | solution.py:52
  240.6 11.8 %copy-start.5 = (s32[1,1,48]{2,1,0:T(1,128)S(1)}, s32[1,1,48]{2,1,0:T(1,128)}, u32[]{:S(2)}) copy-start(s32[1,1,48]{2,1,0:T(1,128)} %param.9) | copy-start | bytes 580
  240.6 105.2 %copy-start.4 = (f32[32768]{0:T(1024)S(1)}, f32[32768]{0:T(1024)}, u32[]{:S(2)}) copy-start(f32[32768]{0:T(1024)} %param.12) | copy-start | bytes 393220
  252.3 187.1 %all-reduce.15.cloned.1.call-start = ((), (), s32[]{:S(2)}) async-start(), calls=%async_computation.3 | async-start | bytes 262144 | tf_op jit(solution)/shard_map/psum | solution.py:53
  345.7 215.9 %all-reduce.17.cloned.1.call-start = ((), (), s32[]{:S(2)}) async-start(), calls=%async_computation.4 | async-start | bytes 262144 | tf_op jit(solution)/shard_map/pmax | solution.py:46
  453.0 219.2 %all-reduce.19.cloned.1.call-start = ((), (), s32[]{:S(2)}) async-start(), calls=%async_computation.5 | async-start | bytes 262144 | tf_op jit(solution)/shard_map/psum | solution.py:47
  563.5 213.0 %all-reduce.21.cloned.1.call-start = ((), (), s32[]{:S(2)}) async-start(), calls=%async_computation.6 | async-start | bytes 262144 | tf_op jit(solution)/shard_map/pmax | solution.py:52
  673.4 105.1 %copy-start.1 = (f32[128,256]{1,0:T(8,128)S(1)}, f32[128,256]{1,0:T(8,128)}, u32[]{:S(2)}) copy-start(f32[128,256]{1,0:T(8,128)} %all-reduce.17.cloned.1.call-done) | copy-start | bytes 393220
  673.4 105.1 %copy-start.2 = (f32[128,256]{1,0:T(8,128)S(1)}, f32[128,256]{1,0:T(8,128)}, u32[]{:S(2)}) copy-start(f32[128,256]{1,0:T(8,128)} %all-reduce.19.cloned.1.call-done) | copy-start | bytes 393220
  685.2 187.3 %all-reduce.23.cloned.1.call-start = ((), (), s32[]{:S(2)}) async-start(), calls=%async_computation.7 | async-start | bytes 262144 | tf_op jit(solution)/shard_map/psum | solution.py:53
Sparse Core Ops, SparseCore 0:
  17.1 111.3 all-reduce.8
  131.6 107.7 all-reduce.10
  252.5 91.1 all-reduce.12
  347.7 91.7 all-reduce.14
  453.1 108.3 all-reduce.16
  564.4 107.7 all-reduce.18
  685.3 91.1 all-reduce.20
  780.7 91.7 all-reduce.22
where the time goes:
time: 882 us; the launch traced here: 881 us
  waiting for transfers between devices  797 us (90%)
  other arithmetic  49.8 us (6%)
  matrix products  15.9 us (2%)
  between operations  15.1 us (2%)
    psum x2, waiting for transfers between devices, settle_rows(): summed = lax.psum(block_sum * jnp.exp(block_max - highest), 'tgt')  217 us
    pmax x2, waiting for transfers between devices, settle_rows(): highest = lax.pmax(block_max, 'tgt')  213 us
    psum x2, waiting for transfers between devices, settle_cols(): summed = lax.psum(block_sum * jnp.exp(block_max - highest), 'src')  187 us
    pmax x2, waiting for transfers between devices, settle_cols(): highest = lax.pmax(block_max, 'src')  180 us
    reduce_sum x4, other arithmetic, tile_partials(): jnp.sum(jnp.exp(shifted - jnp.expand_dims(tile_max, reduce_axis)), axis=r...  22.1 us
    reduce_max x4, other arithmetic, tile_partials(): tile_max = jnp.max(shifted, axis=reduce_axis)  18 us
  transfers between devices with their start and end apart: 8, of which 8 were waited for; matrix products, arithmetic and copies ran while one was open for 1% of the time, Pallas kernels for 0%

commit v1 on v0

v1 whole, which is shorter than its diff:
```python
import functools

import jax
import jax.numpy as jnp
from jax import lax
from jax.experimental import pallas as pl
from jax.experimental.pallas import tpu as pltpu
from jax.sharding import PartitionSpec as P

ITERS = 2
TINY = 1e-37
LOG2E = 1.4426950408889634
LN2 = 0.6931471805599453
MESH = pl.DeviceIdType.MESH
GROUP = 4
CHUNK = 4

SPREAD = 8.0


def lse2(values):
    top = jnp.max(values, axis=0)
    total = jnp.sum(jnp.exp2(values - top[None]), axis=0)
    return top + log2(total)


def membership(ids_ref, count, into, back):
    slots = ids_ref.shape[1]
    block = lax.broadcasted_iota(jnp.int32, (128, slots), 0)
    slot = lax.broadcasted_iota(jnp.int32, (128, slots), 1)
    hit = (ids_ref[...] == block) & (slot < count)
    hit = jnp.where(hit, 1.0, 0.0)
    into[...] = hit.astype(jnp.bfloat16)
    back[...] = hit.T.astype(jnp.bfloat16)


def dot(a, b):
    return jnp.dot(a, b, preferred_element_type=jnp.float32)


def log2(x):
    return jnp.log(x) * LOG2E


def whole(
    n_src, n_tgt,
    k_hbm, rows_ref, cols_ref, count_ref, la_hbm, lb_hbm, g0_hbm,
    f_out, g_out,
    kb, kt, kf, pots, parts, rs_row, rs_col, la_v, lb_v, lb_other, g_own, g_last, g_raw, gathered, wide0, wide1, mrun, srun, f_nat,
    into_r, back_r, into_c, back_c, k_sem, in_sem, out_sem, lb_sem, lb_rsem, rs_send, rs_recv, ag_send, ag_recv,
):
    s, t = lax.axis_index("src"), lax.axis_index("tgt")
    z, c = t // 2, t % 2
    slots = kb.shape[0]
    n_chunks = slots // CHUNK
    n_z = n_tgt // 2
    r_rows = 128 // n_z
    c_rows = 128 // n_src

    def k_copy(i):
        piece = pl.ds(i * CHUNK, CHUNK)
        return pltpu.make_async_copy(k_hbm.at[piece], kb.at[piece], k_sem.at[i])

    g0_copy = pltpu.make_async_copy(g0_hbm, g_raw, in_sem.at[0])
    g0_copy.start()
    la_copy = pltpu.make_async_copy(la_hbm.at[pl.ds(2 * z * r_rows, 2 * r_rows)], la_v, in_sem.at[1])
    la_copy.start()
    lb_copy = pltpu.make_async_copy(lb_hbm.at[pl.ds(2 * s * c_rows, 2 * c_rows)], lb_v, in_sem.at[2])
    lb_copy.start()
    for i in range(n_chunks):
        k_copy(i).start()

    def row_hub(d):
        return (s, 2 * ((z + d) % n_z) + 1)

    def row_low(d):
        return (s, 2 * ((z + d) % n_z))

    def col_hub(d):
        return ((s + d) % n_src, 2 * z + 1)

    def col_low(d):
        return ((s + d) % n_src, 2 * z)

    barrier = pltpu.get_barrier_semaphore()

    def greet(peer):
        pl.semaphore_signal(barrier, inc=1, device_id=peer, device_id_type=MESH)

    @pl.when(c == 1)
    def _():
        for d in range(1, n_z):
            greet(row_hub(d))
            greet(row_low(d))
        for d in range(1, n_src):
            greet(col_hub(d))
            greet(col_low(d))
        greet((s, 2 * z))

    @pl.when(c == 0)
    def _():
        for d in range(1, n_z):
            greet(row_hub(d))
        for d in range(1, n_src):
            greet(col_hub(d))
        greet((s, 2 * z + 1))

    count = count_ref[0, 0]
    membership(rows_ref, count, into_r, back_r)
    membership(cols_ref, count, into_c, back_c)

    def blocks_of(ref, rows):
        return jnp.stack([ref[pl.ds(h, rows, stride=2), :] for h in (0, 1)])

    g0_copy.wait()
    pots[0] = blocks_of(g_raw, 128) * LOG2E
    la_copy.wait()
    lb_copy.wait()

    def prepare(i, carry):
        k_copy(i).wait()
        for u in range(CHUNK):
            slot = i * CHUNK + u
            for p in (0, 1):
                for q in (0, 1):
                    piece = kb[slot, 128 * p : 128 * p + 128, 128 * q : 128 * q + 128]
                    kf[slot, 128 * p : 128 * p + 128, 128 * q : 128 * q + 128] = piece.astype(jnp.float32) * LOG2E
                    flipped = piece.T.astype(jnp.float32) * LOG2E
                    kt[slot, 128 * q : 128 * q + 128, 128 * p : 128 * p + 128] = flipped
        return carry

    def sweep(tiles, pot, pick, into, back, part):
        def widen(wide, slot):
            for u in range(GROUP):
                for q in (0, 1):
                    row = gathered[pl.ds(q * slots + jnp.minimum(slot + u, slots - 1), 1), :]
                    wide[u, 128 * q : 128 * q + 128, :] = jnp.broadcast_to(row, (128, 128)).T

        def add_up(wide, slot, low):
            for u in range(GROUP):
                for h in (0, 1):
                    x = tiles[slot + u, :, 128 * h : 128 * h + 128] + wide[u]
                    x = x.reshape(32, 8, 128)
                    top = jnp.maximum(jnp.max(x, axis=0), mrun[low, :])
                    here = pl.ds(pl.multiple_of((slot + u) * 16 + 8 * h, 8), 8)
                    mrun[here, :] = top
                    srun[here, :] = jnp.sum(jnp.exp2(x - top[None]), axis=0)

        def step(i, carry):
            slot = i * (2 * GROUP)
            low = pl.ds(pl.multiple_of(16 * slots + 8 * jnp.maximum(i - slots, 0), 8), 8)
            widen(wide1, slot + GROUP)
            add_up(wide0, slot, low)
            widen(wide0, slot + 2 * GROUP)
            add_up(wide1, slot + GROUP, low)
            return carry

        mrun[16 * slots : 16 * slots + 8, :] = jnp.full((8, 128), -1e30, jnp.float32)
        value = jnp.concatenate([pot[0], pot[1]], axis=1)
        rows = jnp.zeros((slots, 256), jnp.float32)
        for _ in range(3):
            part_of = value.astype(jnp.bfloat16)
            rows += dot(pick[...], part_of)
            value -= part_of.astype(jnp.float32)
        for q in (0, 1):
            gathered[q * slots : (q + 1) * slots, :] = rows[:, 128 * q : 128 * q + 128]
        widen(wide0, 0)
        lax.fori_loop(0, slots // (2 * GROUP), step, 0)

        def over_sublanes(i, h):
            lines = [pl.ds(128 * i + 8 * h + k, 8, stride=16) for k in range(8)]
            tops = [mrun[p, :] for p in lines]
            top = functools.reduce(jnp.maximum, tops)
            return top + log2(sum(srun[p, :] * jnp.exp2(t - top) for p, t in zip(lines, tops)))

        lse = jnp.concatenate(
            [jnp.concatenate([over_sublanes(i, h) for h in (0, 1)], axis=1) for i in range(slots // 8)], axis=0
        )
        live = lax.broadcasted_iota(jnp.int32, (slots, 256), 0) < count
        lse = jnp.where(live, lse, -2000.0)
        gauge = dot(into[...], jnp.exp2(lse * (1.0 / SPREAD)).astype(jnp.bfloat16))
        level = (SPREAD * log2(gauge + TINY)).astype(jnp.bfloat16)
        scaled = jnp.exp2(lse - dot(back[...], level))
        coarse = scaled.astype(jnp.bfloat16)
        fine = (scaled - coarse.astype(jnp.float32)).astype(jnp.bfloat16)
        total = dot(into[...], coarse) + dot(into[...], fine)
        total = level.astype(jnp.float32) + log2(total + TINY)
        for h in (0, 1):
            part[h] = total[:, 128 * h : 128 * h + 128]

    def remote(src, dst, send, recv, peer):
        pltpu.make_async_remote_copy(
            src_ref=src, dst_ref=dst, send_sem=send, recv_sem=recv, device_id=peer, device_id_type=MESH
        ).start()

    def wait_bytes(ref, sem):
        pltpu.make_async_copy(ref, ref, sem).wait()

    def row_round(it, part, pot):
        rs, rr, gs, gr = rs_send.at[it, 0], rs_recv.at[it, 0], ag_send.at[it, 0], ag_recv.at[it, 0]
        inbox = rs_row.at[it]
        order = sorted(range(1, n_z), key=lambda d: -min(d, n_z - d))

        def share(owner):
            return pl.ds(pl.multiple_of(owner * r_rows, r_rows), r_rows)

        for d in order:
            remote(part.at[:, share((z + d) % n_z), :], inbox.at[t], rs, rr, row_hub(d))
        mine = pot.at[:, share(z), :]

        @pl.when(c == 0)
        def _():
            remote(part.at[:, share(z), :], inbox.at[t], rs, rr, (s, 2 * z + 1))
            wait_bytes(part, rs)
            wait_bytes(pot, gr)

        @pl.when(c == 1)
        def _():
            inbox[t] = part[:, share(z), :]
            wait_bytes(inbox.at[pl.ds(0, n_tgt - 1)], rr)
            mine[...] = blocks_of(la_v, r_rows) * LOG2E - lse2(inbox[...])
            for d in order:
                remote(mine, mine, gs, gr, row_low(d))
                remote(mine, mine, gs, gr, row_hub(d))
            remote(mine, mine, gs, gr, (s, 2 * z))
            wait_bytes(inbox.at[pl.ds(0, n_z - 1)], rs)
            wait_bytes(inbox.at[pl.ds(0, n_z - 1)], gr)
            wait_bytes(inbox.at[pl.ds(0, n_tgt - 1)], gs)

    def far(d):
        y, x = d // 4, d % 4
        return min(y, 4 - y) + min(x, 4 - x)

    def col_round(it, part, pot, last):
        rs, gr = rs_send.at[it, 1], ag_recv.at[it, 1]
        rr = rs_recv.at[it, 1 + c]
        rr_low, rr_high, gs_low, gs_high = [m.at[it, k] for m in (rs_recv, ag_send) for k in (1, 2)]
        inbox = rs_col.at[it]
        order = sorted(range(1, n_src), key=lambda d: -far(d))
        box = inbox.at[c, s]

        def share(owner):
            return part.at[:, pl.ds(pl.multiple_of(owner * c_rows, c_rows), c_rows), :]

        for d in order:
            remote(share((s + d) % n_src), box, rs, rr, col_hub(d))
        if last:
            home = pot.at[pl.ds(pl.multiple_of(s * 2 * c_rows, 2 * c_rows), 2 * c_rows)]
            own = [g_last.at[0], g_last.at[1]]
        else:
            home = pot.at[:, pl.ds(pl.multiple_of(s * c_rows, c_rows), c_rows), :]
            own = [g_own.at[0], g_own.at[1]]

        def settle(core, value):
            if last:
                for h in (0, 1):
                    own[core][pl.ds(h, c_rows, stride=2), :] = value[h] * LN2
            else:
                own[core][...] = value

        @pl.when(c == 0)
        def _():
            remote(share(s), box, rs, rr, (s, 2 * z + 1))
            wait_bytes(part, rs)
            wait_bytes(pot, gr)

        @pl.when(c == 1)
        def _():
            box[...] = share(s)[...]
            wait_bytes(inbox.at[0], rr_low)
            settle(0, blocks_of(lb_other, c_rows) * LOG2E - lse2(inbox[0]))
            for d in order:
                remote(own[0], home, gs_low, gr, col_low(d))
            remote(own[0], home, gs_low, gr, (s, 2 * z))
            wait_bytes(inbox.at[1, pl.ds(0, n_src - 1)], rr_high)
            settle(1, blocks_of(lb_v, c_rows) * LOG2E - lse2(inbox[1]))
            for d in order:
                remote(own[1], home, gs_high, gr, col_hub(d))
            keep = pltpu.make_async_copy(own[1], home, out_sem.at[1])
            keep.start()
            keep.wait()
            wait_bytes(inbox.at[1, pl.ds(0, n_src - 1)], rs)
            wait_bytes(inbox.at[1, pl.ds(0, n_src - 1)], gr)
            wait_bytes(inbox.at[0], gs_low)
            wait_bytes(inbox.at[1, pl.ds(0, n_src - 1)], gs_high)

    lax.fori_loop(0, n_chunks, prepare, 0)
    f_copy = pltpu.make_async_copy(f_nat, f_out, out_sem.at[0])
    for it in range(ITERS):
        sweep(kt, pots.at[2 * it], back_c, into_r, back_r, parts.at[2 * it])
        if it == 0:
            pl.semaphore_wait(barrier, jnp.where(c == 1, 2 * (n_z - 1) + 2 * (n_src - 1) + 1, n_z + n_src - 1))

            @pl.when(c == 0)
            def _():
                lb_remote = pltpu.make_async_remote_copy(
                    src_ref=lb_v, dst_ref=lb_other, send_sem=lb_sem, recv_sem=lb_rsem,
                    device_id=(s, 2 * z + 1), device_id_type=MESH,
                )
                lb_remote.start()
                lb_remote.wait_send()

        row_round(it, parts.at[2 * it], pots.at[2 * it + 1])
        if it == 0:
            @pl.when(c == 1)
            def _():
                wait_bytes(lb_other, lb_rsem)

        if it == ITERS - 1:
            for h in (0, 1):
                f_nat[pl.ds(h, 128, stride=2), :] = pots[2 * it + 1, h] * LN2
            f_copy.start()
        sweep(kf, pots.at[2 * it + 1], back_r, into_c, back_c, parts.at[2 * it + 1])
        last = it == ITERS - 1
        col_round(it, parts.at[2 * it + 1], g_out if last else pots.at[2 * it + 2], last)
    f_copy.wait()


def hand_over(f_in, g_in, f_out, g_out):
    f_out[...] = f_in[...]
    g_out[...] = g_in[...]


def per_device(n_src, n_tgt, log_kernel, tile_rows, tile_cols, tile_count, log_a, log_b, g_start):
    slots, width = log_kernel.shape[2], log_kernel.shape[3]
    f32 = jnp.float32
    anywhere = pl.BlockSpec(memory_space=pl.ANY)
    vmem = pl.BlockSpec(memory_space=pltpu.VMEM)
    smem = pl.BlockSpec(memory_space=pltpu.SMEM)
    r_rows, c_rows = 128 // (n_tgt // 2), 128 // n_src
    dma = pltpu.SemaphoreType.DMA
    f, g = pl.pallas_call(
        functools.partial(whole, n_src, n_tgt),
        out_shape=(jax.ShapeDtypeStruct((256, 128), f32), jax.ShapeDtypeStruct((256, 128), f32)),
        in_specs=[anywhere, vmem, vmem, smem, anywhere, anywhere, anywhere],
        out_specs=(anywhere, anywhere),
        scratch_shapes=[
            pltpu.VMEM((slots, width, width), jnp.bfloat16),
            pltpu.VMEM((slots, width, width), f32),
            pltpu.VMEM((slots, width, width), f32),
            pltpu.VMEM((2 * ITERS, 2, 128, 128), f32),
            pltpu.VMEM((2 * ITERS, 2, 128, 128), f32),
            pltpu.VMEM((ITERS, n_tgt, 2, r_rows, 128), f32),
            pltpu.VMEM((ITERS, 2, n_src, 2, c_rows, 128), f32),
            pltpu.VMEM((2 * r_rows, 128), f32),
            pltpu.VMEM((2 * c_rows, 128), f32),
            pltpu.VMEM((2 * c_rows, 128), f32),
            pltpu.VMEM((2, 2, c_rows, 128), f32),
            pltpu.VMEM((2, 2 * c_rows, 128), f32),
            pltpu.VMEM((256, 128), f32),
            pltpu.VMEM((2 * slots, 128), f32),
            pltpu.VMEM((GROUP, 256, 128), f32),
            pltpu.VMEM((GROUP, 256, 128), f32),
            pltpu.VMEM((16 * slots + 8, 128), f32),
            pltpu.VMEM((16 * slots, 128), f32),
            pltpu.VMEM((256, 128), f32),
            pltpu.VMEM((128, slots), jnp.bfloat16),
            pltpu.VMEM((slots, 128), jnp.bfloat16),
            pltpu.VMEM((128, slots), jnp.bfloat16),
            pltpu.VMEM((slots, 128), jnp.bfloat16),
            dma((slots // CHUNK,)),
            dma((3,)),
            dma((2,)),
            dma,
            dma,
            dma((ITERS, 2)),
            dma((ITERS, 3)),
            dma((ITERS, 3)),
            dma((ITERS, 2)),
        ],
        compiler_params=pltpu.CompilerParams(
            collective_id=0, has_side_effects=True, vmem_limit_bytes=56 * 1024 * 1024
        ),
        name="sinkhorn",
    )(
        log_kernel.reshape(slots, width, width),
        tile_rows.reshape(1, slots),
        tile_cols.reshape(1, slots),
        tile_count,
        log_a.reshape(256, 128),
        log_b.reshape(256, 128),
        g_start.reshape(256, 128),
    )
    f, g = pl.pallas_call(
        hand_over,
        out_shape=(jax.ShapeDtypeStruct((256, 128), f32), jax.ShapeDtypeStruct((256, 128), f32)),
        in_specs=[vmem, vmem],
        out_specs=(vmem, vmem),
        name="hand_over",
    )(f, g)
    return f.reshape(-1), g.reshape(-1)


def solution(mesh):
    n_src, n_tgt = mesh.shape["src"], mesh.shape["tgt"]
    in_specs = (
        P("src", "tgt", None, None, None),
        P("src", "tgt", None),
        P("src", "tgt", None),
        P("src", "tgt"),
        P("src"),
        P("tgt"),
        P("tgt"),
    )
    return jax.shard_map(
        functools.partial(per_device, n_src, n_tgt),
        mesh=mesh, in_specs=in_specs, out_specs=(P("src"), P("tgt")), check_vma=False,
    )
```

time: 882 us -> 72 us (0.08)
  waiting for transfers between devices: 797 us -> 0 us
  Pallas kernels: 0 us -> 70.6 us
  other arithmetic: 49.8 us -> 0 us
  matrix products: 15.9 us -> 0 us
  between operations: 15.1 us -> 1.28 us
    psum x4 -> x0, waiting for transfers between devices: 404 us -> none  [the longest x2 217 us: settle_rows(): summed = lax.psum(block_sum * jnp.exp(block_max - highest), 'tgt')]
    pmax x4 -> x0, waiting for transfers between devices: 393 us -> none  [the longest x2 213 us: settle_rows(): highest = lax.pmax(block_max, 'tgt')]
    pallas_call x0 -> x2, Pallas kernels: none -> 70.6 us  [the longest x1 68.9 us: per_device(): pl.pallas_call(functools.partial(whole, n_src, n_tgt), out_shape=(jax.Sha...]
    reduce_max x8 -> x0, other arithmetic: 25.6 us -> none  [the longest x4 18 us: tile_partials(): tile_max = jnp.max(shifted, axis=reduce_axis)]
    reduce_sum x4 -> x0, other arithmetic: 22.1 us -> none  [tile_partials(): jnp.sum(jnp.exp(shifted - jnp.expand_dims(tile_max, reduce_axis)), axis=r...]
    dot_general x12 -> x0, matrix products: 15.9 us -> none  [the longest x4 7.77 us: fold_blocks(): jnp.einsum('tr,tb->rb', weight, scaled, precision=lax.Precision.HIGHEST)]
  transfers between devices with their start and end apart: 8 -> 0, of which waited for: 8 -> 0; matrix products, arithmetic and copies ran while one was open for 1% -> 0% of each run, Pallas kernels for 0% -> 0%
where the time goes in v1:
time: 72 us; the launch traced here: 71.9 us
  Pallas kernels  70.6 us (98%)
  between operations  1.28 us (2%)
    pallas_call x1, Pallas kernels, per_device(): pl.pallas_call(functools.partial(whole, n_src, n_tgt), out_shape=(jax.Sha...  68.9 us
    pallas_call x1, Pallas kernels, per_device(): pl.pallas_call(hand_over, out_shape=(jax.ShapeDtypeStruct((256, 128), f32...  1.68 us

profile of v1, /device:TPU:1, one launch (start us, length us, event | category | flops | bytes accessed | tf_op | source)
XLA Modules:
  0.0 71.9 jit_solution(3724589756572664643)
XLA Ops:
  1.3 68.9 %sinkhorn.1 = (f32[256,128]{1,0:T(8,128)}, f32[256,128]{1,0:T(8,128)}) custom-call(bf16[48,256,256]{2,1,0:T(8,128)(2,1)} %bitcast.8, s32[1,48]{1,0:T(1,128)} %bitcast.12, s32[1,48]{1,0:T(1,128)} %bitcast.13, s32[1,1]{1,0:T(1,128)S(6)} %copy.9.count_ref, f32[256,128]{1,0:T(8,128)} %bitcast.9, f32[256,128]{1,0:T(8,128)} %bitcast.10, f32[256,128]{1,0:T(8,128)} %bitcast.11), custom_call_target="tpu_custom_call" | custom-call | tf_op jit(solution)/shard_map/sinkhorn/pallas_call | solution.py:332
  70.2 1.7 %hand_over.1 = (f32[256,128]{1,0:T(8,128)}, f32[256,128]{1,0:T(8,128)}) custom-call(f32[256,128]{1,0:T(8,128)} %get-tuple-element.6.f_in, f32[256,128]{1,0:T(8,128)} %get-tuple-element.7.g_in), custom_call_target="tpu_custom_call" | custom-call | tf_op jit(solution)/shard_map/hand_over/pallas_call | solution.py:384

commit v2 on v1

v2 whole, which is shorter than its diff:
```python
import functools

import jax
import jax.numpy as jnp
from jax import lax
from jax.experimental import pallas as pl
from jax.experimental.pallas import tpu as pltpu
from jax.sharding import PartitionSpec as P

ITERS = 2
TINY = 1e-37
LOG2E = 1.4426950408889634
LN2 = 0.6931471805599453
MESH = pl.DeviceIdType.MESH
GROUP = 4
CHUNK = 4

SPREAD = 8.0


def lse2(values):
    top = jnp.max(values, axis=0)
    total = jnp.sum(jnp.exp2(values - top[None]), axis=0)
    return top + log2(total)


def membership(ids_ref, count, into, back):
    slots = ids_ref.shape[1]
    block = lax.broadcasted_iota(jnp.int32, (128, slots), 0)
    slot = lax.broadcasted_iota(jnp.int32, (128, slots), 1)
    hit = (ids_ref[...] == block) & (slot < count)
    hit = jnp.where(hit, 1.0, 0.0)
    into[...] = hit.astype(jnp.bfloat16)
    back[...] = hit.T.astype(jnp.bfloat16)


def dot(a, b):
    return jnp.dot(a, b, preferred_element_type=jnp.float32)


def log2(x):
    return jnp.log(x) * LOG2E


def whole(
    n_src, n_tgt,
    k_hbm, rows_hbm, cols_hbm, count_ref, la_hbm, lb_hbm, g0_hbm,
    f_out, g_out,
    rows_ref, cols_ref, kb, kt, kf, pots, parts, rs_row, rs_col, la_v, lb_v, lb_low, g_low, g_last, g_raw, gathered, wide0, wide1,
    kept, mrun, srun, into_r, back_r, into_c, back_c,
    k_sem, in_sem, out_sem, lb_sem, lb_rsem, rs_send, rs_recv, ag_send, ag_recv,
):
    s, t = lax.axis_index("src"), lax.axis_index("tgt")
    z, c = t // 2, t % 2
    slots = kb.shape[0]
    n_chunks = slots // CHUNK
    n_z = n_tgt // 2
    r_rows = 128 // n_z
    c_rows = 128 // n_src
    low_core = (s, 2 * z)
    hub = (s, 2 * z + 1)

    def k_copy(i):
        piece = pl.ds(i * CHUNK, CHUNK)
        return pltpu.make_async_copy(k_hbm.at[piece], kb.at[piece], k_sem.at[i])

    g0_copy = pltpu.make_async_copy(g0_hbm, g_raw, in_sem.at[0])
    g0_copy.start()
    for i in range(n_chunks):
        k_copy(i).start()
    id_copies = [
        pltpu.make_async_copy(rows_hbm, rows_ref, in_sem.at[3]),
        pltpu.make_async_copy(cols_hbm, cols_ref, in_sem.at[4]),
    ]
    for copy in id_copies:
        copy.start()
    la_copy = pltpu.make_async_copy(la_hbm.at[pl.ds(2 * z * r_rows, 2 * r_rows)], la_v, in_sem.at[1])
    la_copy.start()
    lb_copy = pltpu.make_async_copy(lb_hbm.at[pl.ds(2 * s * c_rows, 2 * c_rows)], lb_v, in_sem.at[2])
    lb_copy.start()

    def row_hub(d):
        return (s, 2 * ((z + d) % n_z) + 1)

    def row_low(d):
        return (s, 2 * ((z + d) % n_z))

    def col_hub(d):
        return ((s + d) % n_src, 2 * z + 1)

    def col_low(d):
        return ((s + d) % n_src, 2 * z)

    barrier = pltpu.get_barrier_semaphore()

    def greet(peer):
        pl.semaphore_signal(barrier, inc=1, device_id=peer, device_id_type=MESH)

    @pl.when(c == 1)
    def _():
        for d in range(1, n_z):
            greet(row_hub(d))
            greet(row_low(d))
        for d in range(1, n_src):
            greet(col_hub(d))
            greet(col_low(d))
        greet(low_core)

    @pl.when(c == 0)
    def _():
        for d in range(1, n_z):
            greet(row_hub(d))
        for d in range(1, n_src):
            greet(col_hub(d))
        greet(hub)

    for copy in id_copies:
        copy.wait()
    count = count_ref[0, 0]
    membership(rows_ref, count, into_r, back_r)
    membership(cols_ref, count, into_c, back_c)

    def blocks_of(ref, rows, h):
        return ref[pl.ds(h, rows, stride=2), :]

    g0_copy.wait()
    for h in (0, 1):
        pots[0, h] = blocks_of(g_raw, 128, h) * LOG2E

    def flip_tiles(i, carry):
        k_copy(i).wait()
        for u in range(CHUNK):
            slot = i * CHUNK + u
            for p in (0, 1):
                for q in (0, 1):
                    piece = kb[slot, 128 * p : 128 * p + 128, 128 * q : 128 * q + 128]
                    flipped = piece.T.astype(jnp.float32) * LOG2E
                    kt[slot, 128 * q : 128 * q + 128, 128 * p : 128 * p + 128] = flipped
        return carry

    def widen_tiles(i, carry):
        for u in range(CHUNK):
            kf[i * CHUNK + u] = kb[i * CHUNK + u].astype(jnp.float32) * LOG2E
        return carry

    def gather(pot, pick):
        value = pot[...]
        rows = jnp.zeros((slots, 128), jnp.float32)
        for _ in range(3):
            piece = value.astype(jnp.bfloat16)
            rows += dot(pick[...], piece)
            value -= piece.astype(jnp.float32)
        gathered[...] = rows

    def spread(wide, slot, keep):
        for u in range(GROUP):
            at = jnp.minimum(slot + u, slots - 1)
            row = jnp.broadcast_to(gathered[pl.ds(at, 1), :], (128, 128)).T
            wide[u] = row
            if keep:
                kept[at] = row

    def add_up(tiles, wide, first, slot, q, halves, guard):
        for u in range(GROUP):
            for h in halves:
                x = tiles[slot + u, 128 * q : 128 * q + 128, 128 * h : 128 * h + 128] + wide[first + u]
                x = x.reshape(16, 8, 128)
                here = pl.ds(pl.multiple_of((slot + u) * 16 + 8 * h, 8), 8)
                old = mrun[guard if q == 0 else here, :]
                top = jnp.maximum(jnp.max(x, axis=0), old)
                mrun[here, :] = top
                total = jnp.sum(jnp.exp2(x - top[None]), axis=0)
                if q == 1:
                    total += srun[here, :] * jnp.exp2(old - top)
                srun[here, :] = total

    def sweep(tiles, q, halves, keep):
        def step(i, carry):
            slot = i * (2 * GROUP)
            guard = pl.ds(pl.multiple_of(16 * slots + 8 * jnp.maximum(i - slots, 0), 8), 8)
            spread(wide1, slot + GROUP, keep)
            add_up(tiles, wide0, 0, slot, q, halves, guard)
            spread(wide0, slot + 2 * GROUP, keep)
            add_up(tiles, wide1, 0, slot + GROUP, q, halves, guard)
            return carry

        spread(wide0, 0, keep)
        lax.fori_loop(0, slots // (2 * GROUP), step, 0)

    def sweep_kept(tiles, q, halves):
        def step(i, carry):
            slot = i * (2 * GROUP)
            add_up(tiles, kept, slot, slot, q, halves, None)
            add_up(tiles, kept, slot + GROUP, slot + GROUP, q, halves, None)
            return carry

        lax.fori_loop(0, slots // (2 * GROUP), step, 0)

    def fold(h, into, back, part):
        def over_sublanes(i):
            lines = [pl.ds(128 * i + 8 * h + k, 8, stride=16) for k in range(8)]
            tops = [mrun[p, :] for p in lines]
            top = functools.reduce(jnp.maximum, tops)
            return top + log2(sum(srun[p, :] * jnp.exp2(m - top) for p, m in zip(lines, tops)))

        lse = jnp.concatenate([over_sublanes(i) for i in range(slots // 8)], axis=0)
        live = lax.broadcasted_iota(jnp.int32, (slots, 128), 0) < count
        lse = jnp.where(live, lse, -2000.0)
        gauge = dot(into[...], jnp.exp2(lse * (1.0 / SPREAD)).astype(jnp.bfloat16))
        level = (SPREAD * log2(gauge + TINY)).astype(jnp.bfloat16)
        scaled = jnp.exp2(lse - dot(back[...], level))
        coarse = scaled.astype(jnp.bfloat16)
        fine = (scaled - coarse.astype(jnp.float32)).astype(jnp.bfloat16)
        total = dot(into[...], coarse) + dot(into[...], fine)
        part[...] = level.astype(jnp.float32) + log2(total + TINY)

    def remote(src, dst, send, recv, peer):
        pltpu.make_async_remote_copy(
            src_ref=src, dst_ref=dst, send_sem=send, recv_sem=recv, device_id=peer, device_id_type=MESH
        ).start()

    def wait_bytes(ref, sem):
        pltpu.make_async_copy(ref, ref, sem).wait()

    def far(d):
        y, x = d // 4, d % 4
        return min(y, 4 - y) + min(x, 4 - x)

    row_order = sorted(range(1, n_z), key=lambda d: -min(d, n_z - d))
    col_order = sorted(range(1, n_src), key=lambda d: -far(d))

    def row_share(ref, owner):
        return ref.at[pl.ds(pl.multiple_of(owner * r_rows, r_rows), r_rows), :]

    def col_share(ref, owner):
        return ref.at[pl.ds(pl.multiple_of(owner * c_rows, c_rows), c_rows), :]

    def send_rows(it, h):
        part, box = parts.at[2 * it, h], rs_row.at[it, h, t]
        sems = rs_send.at[2 * it, h], rs_recv.at[2 * it, h, 0]
        for d in row_order:
            remote(row_share(part, (z + d) % n_z), box, *sems, row_hub(d))

        @pl.when(c == 0)
        def _():
            remote(row_share(part, z), box, *sems, hub)

        @pl.when(c == 1)
        def _():
            box[...] = row_share(part, z)[...]

    def settle_rows(it):
        @pl.when(c == 1)
        def _():
            for h in (0, 1):
                inbox = rs_row.at[it, h]
                mine = row_share(pots.at[2 * it + 1, h], z)
                sems = ag_send.at[2 * it, h, 0], ag_recv.at[2 * it, h]
                wait_bytes(inbox.at[pl.ds(0, n_tgt - 1)], rs_recv.at[2 * it, h, 0])
                mine[...] = blocks_of(la_v, r_rows, h) * LOG2E - lse2(inbox[...])
                for d in row_order:
                    remote(mine, mine, *sems, row_low(d))
                    remote(mine, mine, *sems, row_hub(d))
                remote(mine, mine, *sems, low_core)

    def wait_rows(it, h):
        pot, sem = pots.at[2 * it + 1, h], ag_recv.at[2 * it, h]

        @pl.when(c == 0)
        def _():
            wait_bytes(pot, sem)

        @pl.when(c == 1)
        def _():
            wait_bytes(pot.at[pl.ds(0, (n_z - 1) * r_rows)], sem)

    def send_cols(it, h):
        part, box = parts.at[2 * it + 1, h], rs_col.at[it, h, c, s]
        sems = rs_send.at[2 * it + 1, h], rs_recv.at[2 * it + 1, h, c]
        for d in col_order:
            remote(col_share(part, (s + d) % n_src), box, *sems, col_hub(d))

        @pl.when(c == 0)
        def _():
            remote(col_share(part, s), box, *sems, hub)

        @pl.when(c == 1)
        def _():
            box[...] = col_share(part, s)[...]

    def reduced(it, h, core):
        inbox = rs_col.at[it, h, core]
        sem = rs_recv.at[2 * it + 1, h, core]
        wait_bytes(inbox.at[pl.ds(0, n_src - core)], sem)
        return blocks_of((lb_low, lb_v)[core], c_rows, h) * LOG2E - lse2(inbox[...])

    def settle_cols(it):
        @pl.when(c == 1)
        def _():
            for h in (0, 1):
                there = col_share(pots.at[2 * it + 2, h], s)
                recv = ag_recv.at[2 * it + 1, h]
                low = g_low.at[it, h]
                low[...] = reduced(it, h, 0)
                for d in col_order:
                    remote(low, there, ag_send.at[2 * it + 1, h, 0], recv, col_low(d))
                remote(low, there, ag_send.at[2 * it + 1, h, 0], recv, low_core)
                there[...] = reduced(it, h, 1)
                for d in col_order:
                    remote(there, there, ag_send.at[2 * it + 1, h, 1], recv, col_hub(d))

    def wait_cols(it, h):
        pot, sem = pots.at[2 * it + 2, h], ag_recv.at[2 * it + 1, h]

        @pl.when(c == 0)
        def _():
            wait_bytes(pot, sem)

        @pl.when(c == 1)
        def _():
            wait_bytes(pot.at[pl.ds(0, (n_src - 1) * c_rows)], sem)

    def last_cols(it):
        home = g_out.at[pl.ds(pl.multiple_of(s * 2 * c_rows, 2 * c_rows), 2 * c_rows)]
        recv = ag_recv.at[2 * it + 1, 0]

        @pl.when(c == 1)
        def _():
            for core in (0, 1):
                for h in (0, 1):
                    g_last[core, pl.ds(h, c_rows, stride=2), :] = reduced(it, h, core) * LN2
                send = ag_send.at[2 * it + 1, 0, core]
                for d in col_order:
                    remote(g_last.at[core], home, send, recv, (col_low, col_hub)[core](d))
                if core == 0:
                    remote(g_last.at[0], home, send, recv, low_core)
            keep = pltpu.make_async_copy(g_last.at[1], home, out_sem)
            keep.start()
            keep.wait()
            wait_bytes(g_out.at[pl.ds(0, (n_src - 1) * 2 * c_rows)], recv)

        @pl.when(c == 0)
        def _():
            wait_bytes(g_out, recv)

    mrun[16 * slots : 16 * slots + 8, :] = jnp.full((8, 128), -1e30, jnp.float32)
    lax.fori_loop(0, n_chunks, flip_tiles, 0)
    for it in range(ITERS):
        gather(pots.at[2 * it, 0], back_c) if it == 0 else None
        for q in (0, 1):
            if it > 0:
                wait_cols(it - 1, q)
                gather(pots.at[2 * it, q], back_c)
            elif q == 1:
                gather(pots.at[2 * it, q], back_c)
            sweep(kt, q, (0, 1) if q == 0 else (0,), q == 1)
        fold(0, into_r, back_r, parts.at[2 * it, 0])
        if it == 0:
            pl.semaphore_wait(barrier, jnp.where(c == 1, 2 * (n_z - 1) + 2 * (n_src - 1) + 1, n_z + n_src - 1))
        send_rows(it, 0)
        sweep_kept(kt, 1, (1,))
        fold(1, into_r, back_r, parts.at[2 * it, 1])
        send_rows(it, 1)
        if it == 0:
            la_copy.wait()
            lb_copy.wait()

            @pl.when(c == 0)
            def _():
                remote(lb_v, lb_low, lb_sem, lb_rsem, hub)

            lax.fori_loop(0, n_chunks, widen_tiles, 0)
        settle_rows(it)
        for q in (0, 1):
            wait_rows(it, q)
            gather(pots.at[2 * it + 1, q], back_r)
            sweep(kf, q, (0, 1) if q == 0 else (0,), q == 1)
        fold(0, into_c, back_c, parts.at[2 * it + 1, 0])
        send_cols(it, 0)
        sweep_kept(kf, 1, (1,))
        fold(1, into_c, back_c, parts.at[2 * it + 1, 1])
        send_cols(it, 1)
        if it == 0:
            @pl.when(c == 1)
            def _():
                wait_bytes(lb_low, lb_rsem)

        if it < ITERS - 1:
            settle_cols(it)
    for h in (0, 1):
        f_out[pl.ds(h, 128, stride=2), :] = pots[2 * ITERS - 1, h] * LN2
    last_cols(ITERS - 1)

    for k in range(2 * ITERS):
        for h in (0, 1):
            part, sem = parts.at[k, h], rs_send.at[k, h]
            own_rows = r_rows if k % 2 == 0 else c_rows

            @pl.when(c == 0)
            def _():
                wait_bytes(part, sem)

            @pl.when(c == 1)
            def _():
                wait_bytes(part.at[pl.ds(0, 128 - own_rows)], sem)
                if k % 2 == 0:
                    wait_bytes(rs_row.at[0, 0, pl.ds(0, n_tgt - 1)], ag_send.at[k, h, 0])
                elif k < 2 * ITERS - 1:
                    wait_bytes(rs_col.at[0, 0, 0], ag_send.at[k, h, 0])
                    wait_bytes(rs_col.at[0, 0, 0, pl.ds(0, n_src - 1)], ag_send.at[k, h, 1])
                elif h == 0:
                    wait_bytes(g_out, ag_send.at[k, h, 0])
                    wait_bytes(g_out.at[pl.ds(0, (n_src - 1) * 2 * c_rows)], ag_send.at[k, h, 1])

    @pl.when(c == 0)
    def _():
        wait_bytes(lb_v, lb_sem)


def per_device(n_src, n_tgt, log_kernel, tile_rows, tile_cols, tile_count, log_a, log_b, g_start):
    slots, width = log_kernel.shape[2], log_kernel.shape[3]
    f32 = jnp.float32
    anywhere = pl.BlockSpec(memory_space=pl.ANY)
    vmem = pl.BlockSpec(memory_space=pltpu.VMEM)
    smem = pl.BlockSpec(memory_space=pltpu.SMEM)
    r_rows, c_rows = 128 // (n_tgt // 2), 128 // n_src
    dma = pltpu.SemaphoreType.DMA
    f, g = pl.pallas_call(
        functools.partial(whole, n_src, n_tgt),
        out_shape=(pltpu.VMEM((256, 128), f32), pltpu.VMEM((256, 128), f32)),
        in_specs=[anywhere, anywhere, anywhere, smem, anywhere, anywhere, anywhere],
        out_specs=(vmem, vmem),
        scratch_shapes=[
            pltpu.VMEM((1, slots), jnp.int32),
            pltpu.VMEM((1, slots), jnp.int32),
            pltpu.VMEM((slots, width, width), jnp.bfloat16),
            pltpu.VMEM((slots, width, width), f32),
            pltpu.VMEM((slots, width, width), f32),
            pltpu.VMEM((2 * ITERS, 2, 128, 128), f32),
            pltpu.VMEM((2 * ITERS, 2, 128, 128), f32),
            pltpu.VMEM((ITERS, 2, n_tgt, r_rows, 128), f32),
            pltpu.VMEM((ITERS, 2, 2, n_src, c_rows, 128), f32),
            pltpu.VMEM((2 * r_rows, 128), f32),
            pltpu.VMEM((2 * c_rows, 128), f32),
            pltpu.VMEM((2 * c_rows, 128), f32),
            pltpu.VMEM((ITERS, 2, c_rows, 128), f32),
            pltpu.VMEM((2, 2 * c_rows, 128), f32),
            pltpu.VMEM((256, 128), f32),
            pltpu.VMEM((slots, 128), f32),
            pltpu.VMEM((GROUP, 128, 128), f32),
            pltpu.VMEM((GROUP, 128, 128), f32),
            pltpu.VMEM((slots, 128, 128), f32),
            pltpu.VMEM((16 * slots + 8, 128), f32),
            pltpu.VMEM((16 * slots, 128), f32),
            pltpu.VMEM((128, slots), jnp.bfloat16),
            pltpu.VMEM((slots, 128), jnp.bfloat16),
            pltpu.VMEM((128, slots), jnp.bfloat16),
            pltpu.VMEM((slots, 128), jnp.bfloat16),
            dma((slots // CHUNK,)),
            dma((5,)),
            dma,
            dma,
            dma,
            dma((2 * ITERS, 2)),
            dma((2 * ITERS, 2, 2)),
            dma((2 * ITERS, 2, 2)),
            dma((2 * ITERS, 2)),
        ],
        compiler_params=pltpu.CompilerParams(
            collective_id=0, has_side_effects=True, vmem_limit_bytes=56 * 1024 * 1024
        ),
        name="sinkhorn",
    )(
        log_kernel.reshape(slots, width, width),
        tile_rows.reshape(1, slots),
        tile_cols.reshape(1, slots),
        tile_count,
        log_a.reshape(256, 128),
        log_b.reshape(256, 128),
        g_start.reshape(256, 128),
    )
    return f.reshape(-1), g.reshape(-1)


def solution(mesh):
    n_src, n_tgt = mesh.shape["src"], mesh.shape["tgt"]
    in_specs = (
        P("src", "tgt", None, None, None),
        P("src", "tgt", None),
        P("src", "tgt", None),
        P("src", "tgt"),
        P("src"),
        P("tgt"),
        P("tgt"),
    )
    return jax.shard_map(
        functools.partial(per_device, n_src, n_tgt),
        mesh=mesh, in_specs=in_specs, out_specs=(P("src"), P("tgt")), check_vma=False,
    )
```

time: 72 us -> 67.2 us (0.933)
  Pallas kernels: 70.6 us -> 64.5 us
  local copies, waits for them, and re-layouts: 0 us -> 1.33 us
    pallas_call x2 -> x1, Pallas kernels: 70.6 us -> 64.5 us  [per_device(): pl.pallas_call(functools.partial(whole, n_src, n_tgt), out_shape=(pltpu.V...]
    unnamed x0 -> x2, local copies, waits for them, and re-layouts: none -> 1.33 us
where the time goes in v2:
time: 67.2 us; the launch traced here: 67.1 us
  Pallas kernels  64.5 us (96%)
  local copies, waits for them, and re-layouts  1.33 us (2%)
  between operations  1.29 us (2%)
    pallas_call x1, Pallas kernels, per_device(): pl.pallas_call(functools.partial(whole, n_src, n_tgt), out_shape=(pltpu.V...  64.5 us

profile of v2, /device:TPU:1, one launch (start us, length us, event | category | flops | bytes accessed | tf_op | source)
XLA Modules:
  0.0 67.1 jit_solution(6152452763513587692)
XLA Ops:
  1.3 64.5 %sinkhorn.1 = (f32[256,128]{1,0:T(8,128)S(1)}, f32[256,128]{1,0:T(8,128)S(1)}) custom-call(bf16[48,256,256]{2,1,0:T(8,128)(2,1)} %bitcast.10, s32[1,48]{1,0:T(1,128)} %bitcast.14, s32[1,48]{1,0:T(1,128)} %bitcast.15, s32[1,1]{1,0:T(1,128)S(6)} %copy.13.count_ref, f32[256,128]{1,0:T(8,128)} %bitcast.11, f32[256,128]{1,0:T(8,128)} %bitcast.12, f32[256,128]{1,0:T(8,128)} %bitcast.13), custom_call_target="tpu_custom_call" | custom-call | tf_op jit(solution)/shard_map/sinkhorn/pallas_call | solution.py:428
  65.8 0.7 copy.11
  66.5 0.7 copy.12

commit v3 on v2

--- a/solution.py
+++ b/solution.py
@@ -12,7 +12,7 @@
 LOG2E = 1.4426950408889634
 LN2 = 0.6931471805599453
 MESH = pl.DeviceIdType.MESH
-GROUP = 4
+GROUP = 6
 CHUNK = 4
 
 SPREAD = 8.0
@@ -47,7 +47,7 @@
     k_hbm, rows_hbm, cols_hbm, count_ref, la_hbm, lb_hbm, g0_hbm,
     f_out, g_out,
     rows_ref, cols_ref, kb, kt, kf, pots, parts, rs_row, rs_col, la_v, lb_v, lb_low, g_low, g_last, g_raw, gathered, wide0, wide1,
-    kept, mrun, srun, into_r, back_r, into_c, back_c,
+    kept0, kept, mrun, srun, into_r, back_r, into_c, back_c,
     k_sem, in_sem, out_sem, lb_sem, lb_rsem, rs_send, rs_recv, ag_send, ag_recv,
 ):
     s, t = lax.axis_index("src"), lax.axis_index("tgt")
@@ -55,8 +55,15 @@
     slots = kb.shape[0]
     n_chunks = slots // CHUNK
     n_z = n_tgt // 2
-    r_rows = 128 // n_z
-    c_rows = 128 // n_src
+    r_shares, c_shares = n_z, n_src // 2
+    r_rows, c_rows = 128 // r_shares, 128 // c_shares
+    side = 4
+    y, x = s // side, s % side
+
+    def col_share_of(y, x):
+        return (y % 2) * side + (x + 2 * (y // 2)) % side
+
+    r_mine, c_mine = z % r_shares, col_share_of(y, x)
     low_core = (s, 2 * z)
     hub = (s, 2 * z + 1)
 
@@ -74,9 +81,9 @@
     ]
     for copy in id_copies:
         copy.start()
-    la_copy = pltpu.make_async_copy(la_hbm.at[pl.ds(2 * z * r_rows, 2 * r_rows)], la_v, in_sem.at[1])
+    la_copy = pltpu.make_async_copy(la_hbm.at[pl.ds(2 * r_mine * r_rows, 2 * r_rows)], la_v, in_sem.at[1])
     la_copy.start()
-    lb_copy = pltpu.make_async_copy(lb_hbm.at[pl.ds(2 * s * c_rows, 2 * c_rows)], lb_v, in_sem.at[2])
+    lb_copy = pltpu.make_async_copy(lb_hbm.at[pl.ds(2 * c_mine * c_rows, 2 * c_rows)], lb_v, in_sem.at[2])
     lb_copy.start()
 
     def row_hub(d):
@@ -85,11 +92,23 @@
     def row_low(d):
         return (s, 2 * ((z + d) % n_z))
 
+    def torus(d):
+        return (y + d[0]) % side, (x + d[1]) % side
+
     def col_hub(d):
-        return ((s + d) % n_src, 2 * z + 1)
+        return (torus(d)[0] * side + torus(d)[1], 2 * z + 1)
 
     def col_low(d):
-        return ((s + d) % n_src, 2 * z)
+        return (torus(d)[0] * side + torus(d)[1], 2 * z)
+
+    def around(d):
+        return min(d, side - d)
+
+    row_order = sorted(range(1, n_z), key=lambda d: -min(d, n_z - d))
+    row_near = row_order
+    col_order = [(dy, dx) for dy in range(side) for dx in range(side) if dy or dx]
+    col_order.sort(key=lambda d: -around(d[0]) - around(d[1]))
+    col_near = ((0, 2), (1, 1), (1, 3), (0, 1), (0, 3), (1, 0), (3, 0))
 
     barrier = pltpu.get_barrier_semaphore()
 
@@ -101,7 +120,7 @@
         for d in range(1, n_z):
             greet(row_hub(d))
             greet(row_low(d))
-        for d in range(1, n_src):
+        for d in col_order:
             greet(col_hub(d))
             greet(col_low(d))
         greet(low_core)
@@ -110,7 +129,7 @@
     def _():
         for d in range(1, n_z):
             greet(row_hub(d))
-        for d in range(1, n_src):
+        for d in col_order:
             greet(col_hub(d))
         greet(hub)
 
@@ -127,71 +146,98 @@
     for h in (0, 1):
         pots[0, h] = blocks_of(g_raw, 128, h) * LOG2E
 
-    def flip_tiles(i, carry):
-        k_copy(i).wait()
-        for u in range(CHUNK):
-            slot = i * CHUNK + u
-            for p in (0, 1):
-                for q in (0, 1):
-                    piece = kb[slot, 128 * p : 128 * p + 128, 128 * q : 128 * q + 128]
-                    flipped = piece.T.astype(jnp.float32) * LOG2E
-                    kt[slot, 128 * q : 128 * q + 128, 128 * p : 128 * p + 128] = flipped
-        return carry
+    def flip(slot):
+        for p in (0, 1):
+            for q in (0, 1):
+                piece = kb[slot, 128 * p : 128 * p + 128, 128 * q : 128 * q + 128]
+                flipped = piece.T.astype(jnp.float32) * LOG2E
+                kt[slot, 128 * q : 128 * q + 128, 128 * p : 128 * p + 128] = flipped
 
     def widen_tiles(i, carry):
         for u in range(CHUNK):
             kf[i * CHUNK + u] = kb[i * CHUNK + u].astype(jnp.float32) * LOG2E
         return carry
 
-    def gather(pot, pick):
+    def gather(pot, pick, q):
         value = pot[...]
         rows = jnp.zeros((slots, 128), jnp.float32)
         for _ in range(3):
             piece = value.astype(jnp.bfloat16)
             rows += dot(pick[...], piece)
             value -= piece.astype(jnp.float32)
-        gathered[...] = rows
-
-    def spread(wide, slot, keep):
-        for u in range(GROUP):
-            at = jnp.minimum(slot + u, slots - 1)
-            row = jnp.broadcast_to(gathered[pl.ds(at, 1), :], (128, 128)).T
+        gathered[q] = rows
+
+    def spread(q, slot, *places):
+        row = jnp.broadcast_to(gathered[q, pl.ds(slot, 1), :], (128, 128)).T
+        for wide, u in places:
             wide[u] = row
-            if keep:
-                kept[at] = row
-
-    def add_up(tiles, wide, first, slot, q, halves, guard):
-        for u in range(GROUP):
-            for h in halves:
-                x = tiles[slot + u, 128 * q : 128 * q + 128, 128 * h : 128 * h + 128] + wide[first + u]
-                x = x.reshape(16, 8, 128)
-                here = pl.ds(pl.multiple_of((slot + u) * 16 + 8 * h, 8), 8)
-                old = mrun[guard if q == 0 else here, :]
-                top = jnp.maximum(jnp.max(x, axis=0), old)
-                mrun[here, :] = top
-                total = jnp.sum(jnp.exp2(x - top[None]), axis=0)
-                if q == 1:
-                    total += srun[here, :] * jnp.exp2(old - top)
-                srun[here, :] = total
+
+    def add_up(tiles, wide, u, slot, q, halves, guard):
+        for h in halves:
+            x = tiles[slot, 128 * q : 128 * q + 128, 128 * h : 128 * h + 128] + wide[u]
+            x = x.reshape(16, 8, 128)
+            here = pl.ds(pl.multiple_of(slot * 16 + 8 * h, 8), 8)
+            old = mrun[guard if q == 0 else here, :]
+            top = jnp.maximum(jnp.max(x, axis=0), old)
+            mrun[here, :] = top
+            total = jnp.sum(jnp.exp2(x - top[None]), axis=0)
+            if q == 1:
+                total += srun[here, :] * jnp.exp2(old - top)
+            srun[here, :] = total
+
+    def guard_of(i):
+        return pl.ds(pl.multiple_of(16 * slots + 8 * jnp.maximum(i - slots, 0), 8), 8)
 
     def sweep(tiles, q, halves, keep):
+        def ahead(wide, u, slot):
+            at = jnp.minimum(slot, slots - 1)
+            spread(q, at, (wide, u), *([(kept, at)] if keep else []))
+
         def step(i, carry):
             slot = i * (2 * GROUP)
-            guard = pl.ds(pl.multiple_of(16 * slots + 8 * jnp.maximum(i - slots, 0), 8), 8)
-            spread(wide1, slot + GROUP, keep)
-            add_up(tiles, wide0, 0, slot, q, halves, guard)
-            spread(wide0, slot + 2 * GROUP, keep)
-            add_up(tiles, wide1, 0, slot + GROUP, q, halves, guard)
+            guard = guard_of(i)
+            for u in range(GROUP):
+                add_up(tiles, wide0, u, slot + u, q, halves, guard)
+                ahead(wide1, u, slot + GROUP + u)
+            for u in range(GROUP):
+                add_up(tiles, wide1, u, slot + GROUP + u, q, halves, guard)
+                ahead(wide0, u, slot + 2 * GROUP + u)
             return carry
 
-        spread(wide0, 0, keep)
+        for u in range(GROUP):
+            ahead(wide0, u, u)
         lax.fori_loop(0, slots // (2 * GROUP), step, 0)
+
+    def first_sweep():
+        def ahead(slot):
+            flip(slot)
+            spread(0, slot, (kept0, slot))
+            spread(1, slot, (kept, slot))
+
+        def add(i, u):
+            slot = i * CHUNK + u
+            add_up(kt, kept0, slot, slot, 0, (0, 1), guard_of(i))
+            add_up(kt, kept, slot, slot, 1, (0,), None)
+
+        def step(i, carry):
+            k_copy(i + 1).wait()
+            for u in range(CHUNK):
+                add(i, u)
+                ahead((i + 1) * CHUNK + u)
+            return carry
+
+        k_copy(0).wait()
+        for u in range(CHUNK):
+            ahead(u)
+        lax.fori_loop(0, n_chunks - 1, step, 0)
+        for u in range(CHUNK):
+            add(n_chunks - 1, u)
 
     def sweep_kept(tiles, q, halves):
         def step(i, carry):
-            slot = i * (2 * GROUP)
-            add_up(tiles, kept, slot, slot, q, halves, None)
-            add_up(tiles, kept, slot + GROUP, slot + GROUP, q, halves, None)
+            for u in range(2 * GROUP):
+                slot = i * (2 * GROUP) + u
+                add_up(tiles, kept, slot, slot, q, halves, None)
             return carry
 
         lax.fori_loop(0, slots // (2 * GROUP), step, 0)
@@ -222,13 +268,6 @@
     def wait_bytes(ref, sem):
         pltpu.make_async_copy(ref, ref, sem).wait()
 
-    def far(d):
-        y, x = d // 4, d % 4
-        return min(y, 4 - y) + min(x, 4 - x)
-
-    row_order = sorted(range(1, n_z), key=lambda d: -min(d, n_z - d))
-    col_order = sorted(range(1, n_src), key=lambda d: -far(d))
-
     def row_share(ref, owner):
         return ref.at[pl.ds(pl.multiple_of(owner * r_rows, r_rows), r_rows), :]
 
@@ -239,26 +278,26 @@
         part, box = parts.at[2 * it, h], rs_row.at[it, h, t]
         sems = rs_send.at[2 * it, h], rs_recv.at[2 * it, h, 0]
         for d in row_order:
-            remote(row_share(part, (z + d) % n_z), box, *sems, row_hub(d))
+            remote(row_share(part, (z + d) % r_shares), box, *sems, row_hub(d))
 
         @pl.when(c == 0)
         def _():
-            remote(row_share(part, z), box, *sems, hub)
-
-        @pl.when(c == 1)
-        def _():
-            box[...] = row_share(part, z)[...]
+            remote(row_share(part, r_mine), box, *sems, hub)
+
+        @pl.when(c == 1)
+        def _():
+            box[...] = row_share(part, r_mine)[...]
 
     def settle_rows(it):
         @pl.when(c == 1)
         def _():
             for h in (0, 1):
                 inbox = rs_row.at[it, h]
-                mine = row_share(pots.at[2 * it + 1, h], z)
+                mine = row_share(pots.at[2 * it + 1, h], r_mine)
                 sems = ag_send.at[2 * it, h, 0], ag_recv.at[2 * it, h]
                 wait_bytes(inbox.at[pl.ds(0, n_tgt - 1)], rs_recv.at[2 * it, h, 0])
                 mine[...] = blocks_of(la_v, r_rows, h) * LOG2E - lse2(inbox[...])
-                for d in row_order:
+                for d in row_near:
                     remote(mine, mine, *sems, row_low(d))
                     remote(mine, mine, *sems, row_hub(d))
                 remote(mine, mine, *sems, low_core)
@@ -272,21 +311,21 @@
 
         @pl.when(c == 1)
         def _():
-            wait_bytes(pot.at[pl.ds(0, (n_z - 1) * r_rows)], sem)
+            wait_bytes(pot.at[pl.ds(0, 128 - r_rows)], sem)
 
     def send_cols(it, h):
         part, box = parts.at[2 * it + 1, h], rs_col.at[it, h, c, s]
         sems = rs_send.at[2 * it + 1, h], rs_recv.at[2 * it + 1, h, c]
         for d in col_order:
-            remote(col_share(part, (s + d) % n_src), box, *sems, col_hub(d))
+            remote(col_share(part, col_share_of(*torus(d))), box, *sems, col_hub(d))
 
         @pl.when(c == 0)
         def _():
-            remote(col_share(part, s), box, *sems, hub)
-
-        @pl.when(c == 1)
-        def _():
-            box[...] = col_share(part, s)[...]
+            remote(col_share(part, c_mine), box, *sems, hub)
+
+        @pl.when(c == 1)
+        def _():
+            box[...] = col_share(part, c_mine)[...]
 
     def reduced(it, h, core):
         inbox = rs_col.at[it, h, core]
@@ -298,15 +337,15 @@
         @pl.when(c == 1)
         def _():
             for h in (0, 1):
-                there = col_share(pots.at[2 * it + 2, h], s)
+                there = col_share(pots.at[2 * it + 2, h], c_mine)
                 recv = ag_recv.at[2 * it + 1, h]
                 low = g_low.at[it, h]
                 low[...] = reduced(it, h, 0)
-                for d in col_order:
+                for d in col_near:
                     remote(low, there, ag_send.at[2 * it + 1, h, 0], recv, col_low(d))
                 remote(low, there, ag_send.at[2 * it + 1, h, 0], recv, low_core)
                 there[...] = reduced(it, h, 1)
-                for d in col_order:
+                for d in col_near:
                     remote(there, there, ag_send.at[2 * it + 1, h, 1], recv, col_hub(d))
 
     def wait_cols(it, h):
@@ -318,10 +357,10 @@
 
         @pl.when(c == 1)
         def _():
-            wait_bytes(pot.at[pl.ds(0, (n_src - 1) * c_rows)], sem)
+            wait_bytes(pot.at[pl.ds(0, 128 - c_rows)], sem)
 
     def last_cols(it):
-        home = g_out.at[pl.ds(pl.multiple_of(s * 2 * c_rows, 2 * c_rows), 2 * c_rows)]
+        home = g_out.at[pl.ds(pl.multiple_of(c_mine * 2 * c_rows, 2 * c_rows), 2 * c_rows)]
         recv = ag_recv.at[2 * it + 1, 0]
 
         @pl.when(c == 1)
@@ -330,30 +369,29 @@
                 for h in (0, 1):
                     g_last[core, pl.ds(h, c_rows, stride=2), :] = reduced(it, h, core) * LN2
                 send = ag_send.at[2 * it + 1, 0, core]
-                for d in col_order:
+                for d in col_near:
                     remote(g_last.at[core], home, send, recv, (col_low, col_hub)[core](d))
                 if core == 0:
                     remote(g_last.at[0], home, send, recv, low_core)
             keep = pltpu.make_async_copy(g_last.at[1], home, out_sem)
             keep.start()
             keep.wait()
-            wait_bytes(g_out.at[pl.ds(0, (n_src - 1) * 2 * c_rows)], recv)
+            wait_bytes(g_out.at[pl.ds(0, 256 - 2 * c_rows)], recv)
 
         @pl.when(c == 0)
         def _():
             wait_bytes(g_out, recv)
 
     mrun[16 * slots : 16 * slots + 8, :] = jnp.full((8, 128), -1e30, jnp.float32)
-    lax.fori_loop(0, n_chunks, flip_tiles, 0)
     for it in range(ITERS):
-        gather(pots.at[2 * it, 0], back_c) if it == 0 else None
         for q in (0, 1):
             if it > 0:
                 wait_cols(it - 1, q)
-                gather(pots.at[2 * it, q], back_c)
-            elif q == 1:
-                gather(pots.at[2 * it, q], back_c)
-            sweep(kt, q, (0, 1) if q == 0 else (0,), q == 1)
+            gather(pots.at[2 * it, q], back_c, q)
+            if it > 0:
+                sweep(kt, q, (0, 1) if q == 0 else (0,), q == 1)
+        if it == 0:
+            first_sweep()
         fold(0, into_r, back_r, parts.at[2 * it, 0])
         if it == 0:
             pl.semaphore_wait(barrier, jnp.where(c == 1, 2 * (n_z - 1) + 2 * (n_src - 1) + 1, n_z + n_src - 1))
@@ -373,7 +411,7 @@
         settle_rows(it)
         for q in (0, 1):
             wait_rows(it, q)
-            gather(pots.at[2 * it + 1, q], back_r)
+            gather(pots.at[2 * it + 1, q], back_r, q)
             sweep(kf, q, (0, 1) if q == 0 else (0,), q == 1)
         fold(0, into_c, back_c, parts.at[2 * it + 1, 0])
         send_cols(it, 0)
@@ -393,24 +431,26 @@
 
     for k in range(2 * ITERS):
         for h in (0, 1):
-            part, sem = parts.at[k, h], rs_send.at[k, h]
-            own_rows = r_rows if k % 2 == 0 else c_rows
+            sem, sent = rs_send.at[k, h], ag_send.at[k, h, 0]
+            rows, cols = rs_row.at[0, 0], rs_col.at[0, 0, 0]
 
             @pl.when(c == 0)
             def _():
-                wait_bytes(part, sem)
+                wait_bytes(rows.at[pl.ds(0, n_z)] if k % 2 == 0 else cols, sem)
 
             @pl.when(c == 1)
             def _():
-                wait_bytes(part.at[pl.ds(0, 128 - own_rows)], sem)
                 if k % 2 == 0:
-                    wait_bytes(rs_row.at[0, 0, pl.ds(0, n_tgt - 1)], ag_send.at[k, h, 0])
-                elif k < 2 * ITERS - 1:
-                    wait_bytes(rs_col.at[0, 0, 0], ag_send.at[k, h, 0])
-                    wait_bytes(rs_col.at[0, 0, 0, pl.ds(0, n_src - 1)], ag_send.at[k, h, 1])
+                    wait_bytes(rows.at[pl.ds(0, n_z - 1)], sem)
+                    wait_bytes(rows.at[pl.ds(0, 2 * len(row_near) + 1)], sent)
+                    return
+                wait_bytes(cols.at[pl.ds(0, n_src - 1)], sem)
+                if k < 2 * ITERS - 1:
+                    wait_bytes(cols.at[pl.ds(0, len(col_near) + 1)], sent)
+                    wait_bytes(cols.at[pl.ds(0, len(col_near))], ag_send.at[k, h, 1])
                 elif h == 0:
-                    wait_bytes(g_out, ag_send.at[k, h, 0])
-                    wait_bytes(g_out.at[pl.ds(0, (n_src - 1) * 2 * c_rows)], ag_send.at[k, h, 1])
+                    wait_bytes(g_out, sent)
+                    wait_bytes(g_out.at[pl.ds(0, 256 - 2 * c_rows)], ag_send.at[k, h, 1])
 
     @pl.when(c == 0)
     def _():
@@ -423,7 +463,7 @@
     anywhere = pl.BlockSpec(memory_space=pl.ANY)
     vmem = pl.BlockSpec(memory_space=pltpu.VMEM)
     smem = pl.BlockSpec(memory_space=pltpu.SMEM)
-    r_rows, c_rows = 128 // (n_tgt // 2), 128 // n_src
+    r_rows, c_rows = 128 // (n_tgt // 2), 128 // (n_src // 2)
     dma = pltpu.SemaphoreType.DMA
     f, g = pl.pallas_call(
         functools.partial(whole, n_src, n_tgt),
@@ -446,9 +486,10 @@
             pltpu.VMEM((ITERS, 2, c_rows, 128), f32),
             pltpu.VMEM((2, 2 * c_rows, 128), f32),
             pltpu.VMEM((256, 128), f32),
-            pltpu.VMEM((slots, 128), f32),
+            pltpu.VMEM((2, slots, 128), f32),
             pltpu.VMEM((GROUP, 128, 128), f32),
             pltpu.VMEM((GROUP, 128, 128), f32),
+            pltpu.VMEM((slots, 128, 128), f32),
             pltpu.VMEM((slots, 128, 128), f32),
             pltpu.VMEM((16 * slots + 8, 128), f32),
             pltpu.VMEM((16 * slots, 128), f32),

time: 67.2 us -> 65.7 us (0.978)
  Pallas kernels: 64.5 us -> 63 us
    pallas_call x1, Pallas kernels: 64.5 us -> 63 us  [per_device(): pl.pallas_call(functools.partial(whole, n_src, n_tgt), out_shape=(pltpu.V...]
where the time goes in v3:
time: 65.7 us; the launch traced here: 65.6 us
  Pallas kernels  63 us (96%)
  local copies, waits for them, and re-layouts  1.33 us (2%)
  between operations  1.29 us (2%)
    pallas_call x1, Pallas kernels, per_device(): pl.pallas_call(functools.partial(whole, n_src, n_tgt), out_shape=(pltpu.V...  63 us
    unnamed x2, local copies, waits for them, and re-layouts  1.33 us

profile of v3, /device:TPU:1, one launch (start us, length us, event | category | flops | bytes accessed | tf_op | source)
XLA Modules:
  0.0 65.6 jit_solution(9526156530974757176)
XLA Ops:
  1.3 63.0 %sinkhorn.1 = (f32[256,128]{1,0:T(8,128)S(1)}, f32[256,128]{1,0:T(8,128)S(1)}) custom-call(bf16[48,256,256]{2,1,0:T(8,128)(2,1)} %bitcast.10, s32[1,48]{1,0:T(1,128)} %bitcast.14, s32[1,48]{1,0:T(1,128)} %bitcast.15, s32[1,1]{1,0:T(1,128)S(6)} %copy.13.count_ref, f32[256,128]{1,0:T(8,128)} %bitcast.11, f32[256,128]{1,0:T(8,128)} %bitcast.12, f32[256,128]{1,0:T(8,128)} %bitcast.13), custom_call_target="tpu_custom_call" | custom-call | tf_op jit(solution)/shard_map/sinkhorn/pallas_call | solution.py:468
  64.3 0.7 %copy.11 = f32[32768]{0:T(1024)} copy(f32[32768]{0:T(1024)S(1)} %bitcast.9) | data formatting | bytes 262144
  64.9 0.7 %copy.12 = f32[32768]{0:T(1024)} copy(f32[32768]{0:T(1024)S(1)} %bitcast.8) | data formatting | bytes 262144

commit v4 on v3

--- a/solution.py
+++ b/solution.py
@@ -188,12 +188,16 @@
     def guard_of(i):
         return pl.ds(pl.multiple_of(16 * slots + 8 * jnp.maximum(i - slots, 0), 8), 8)
 
-    def sweep(tiles, q, halves, keep):
+    rounds = slots // (2 * GROUP)
+
+    def sweep(tiles, q):
+        keep = (kept0, kept)[q]
+
         def ahead(wide, u, slot):
             at = jnp.minimum(slot, slots - 1)
-            spread(q, at, (wide, u), *([(kept, at)] if keep else []))
-
-        def step(i, carry):
+            spread(q, at, (wide, u), (keep, at))
+
+        def step(halves, i, carry):
             slot = i * (2 * GROUP)
             guard = guard_of(i)
             for u in range(GROUP):
@@ -206,7 +210,10 @@
 
         for u in range(GROUP):
             ahead(wide0, u, u)
-        lax.fori_loop(0, slots // (2 * GROUP), step, 0)
+        middle = rounds // 2 if q == 0 else 0
+        if middle:
+            lax.fori_loop(0, middle, functools.partial(step, (0, 1)), 0)
+        lax.fori_loop(middle, rounds, functools.partial(step, (0,)), 0)
 
     def first_sweep():
         def ahead(slot):
@@ -233,14 +240,19 @@
         for u in range(CHUNK):
             add(n_chunks - 1, u)
 
-    def sweep_kept(tiles, q, halves):
-        def step(i, carry):
+    def sweep_kept(tiles, rest):
+        def step(late, i, carry):
             for u in range(2 * GROUP):
                 slot = i * (2 * GROUP) + u
-                add_up(tiles, kept, slot, slot, q, halves, None)
+                if late:
+                    add_up(tiles, kept0, slot, slot, 0, (1,), guard_of(i))
+                add_up(tiles, kept, slot, slot, 1, (1,), None)
             return carry
 
-        lax.fori_loop(0, slots // (2 * GROUP), step, 0)
+        middle = rounds // 2 if rest else rounds
+        lax.fori_loop(0, middle, functools.partial(step, False), 0)
+        if rest:
+            lax.fori_loop(middle, rounds, functools.partial(step, True), 0)
 
     def fold(h, into, back, part):
         def over_sublanes(i):
@@ -389,14 +401,14 @@
                 wait_cols(it - 1, q)
             gather(pots.at[2 * it, q], back_c, q)
             if it > 0:
-                sweep(kt, q, (0, 1) if q == 0 else (0,), q == 1)
+                sweep(kt, q)
         if it == 0:
             first_sweep()
         fold(0, into_r, back_r, parts.at[2 * it, 0])
         if it == 0:
             pl.semaphore_wait(barrier, jnp.where(c == 1, 2 * (n_z - 1) + 2 * (n_src - 1) + 1, n_z + n_src - 1))
         send_rows(it, 0)
-        sweep_kept(kt, 1, (1,))
+        sweep_kept(kt, it > 0)
         fold(1, into_r, back_r, parts.at[2 * it, 1])
         send_rows(it, 1)
         if it == 0:
@@ -412,10 +424,10 @@
         for q in (0, 1):
             wait_rows(it, q)
             gather(pots.at[2 * it + 1, q], back_r, q)
-            sweep(kf, q, (0, 1) if q == 0 else (0,), q == 1)
+            sweep(kf, q)
         fold(0, into_c, back_c, parts.at[2 * it + 1, 0])
         send_cols(it, 0)
-        sweep_kept(kf, 1, (1,))
+        sweep_kept(kf, True)
         fold(1, into_c, back_c, parts.at[2 * it + 1, 1])
         send_cols(it, 1)
         if it == 0:

time: 65.7 us -> 65.7 us (level)
  no operation moved by 1% of the time
where the time goes in v4:
time: 65.7 us; the launch traced here: 65.6 us
  Pallas kernels  63 us (96%)
  local copies, waits for them, and re-layouts  1.33 us (2%)
  between operations  1.29 us (2%)
    pallas_call x1, Pallas kernels, per_device(): pl.pallas_call(functools.partial(whole, n_src, n_tgt), out_shape=(pltpu.V...  63 us
    unnamed x2, local copies, waits for them, and re-layouts  1.33 us

profile of v4, /device:TPU:1, one launch (start us, length us, event | category | flops | bytes accessed | tf_op | source)
XLA Modules:
  0.0 65.6 jit_solution(13888461274003179675)
XLA Ops:
  1.3 63.0 %sinkhorn.1 = (f32[256,128]{1,0:T(8,128)S(1)}, f32[256,128]{1,0:T(8,128)S(1)}) custom-call(bf16[48,256,256]{2,1,0:T(8,128)(2,1)} %bitcast.10, s32[1,48]{1,0:T(1,128)} %bitcast.14, s32[1,48]{1,0:T(1,128)} %bitcast.15, s32[1,1]{1,0:T(1,128)S(6)} %copy.13.count_ref, f32[256,128]{1,0:T(8,128)} %bitcast.11, f32[256,128]{1,0:T(8,128)} %bitcast.12, f32[256,128]{1,0:T(8,128)} %bitcast.13), custom_call_target="tpu_custom_call" | custom-call | tf_op jit(solution)/shard_map/sinkhorn/pallas_call | solution.py:480
  64.3 0.7 %copy.11 = f32[32768]{0:T(1024)} copy(f32[32768]{0:T(1024)S(1)} %bitcast.9) | data formatting | bytes 262144
  65.0 0.7 %copy.12 = f32[32768]{0:T(1024)} copy(f32[32768]{0:T(1024)S(1)} %bitcast.8) | data formatting | bytes 262144
